TPU v7x, 128 devices: a whole 4x4x4 slice. The times are simulated.
128 devices in a mesh: ex: 16 (over y, x), lay: 8 (over z, core).
Axes of the slice: x: 4, y: 4, z: 4, core: 2. Of those that a mesh axis runs over, the one named last changes fastest.
Arguments:
- grads: bfloat16 [8, 16384, 4096], P('lay', 'ex'), may hold values from -0.119628906 to 0.119628906
- prec_in: bfloat16 [8, 64, 64], P('lay'), as said below
- prec_out: bfloat16 [8, 64, 64], P('lay'), as said below
- requests: int32 [16, 16], replicated, may hold values from 0 to 7
- pairs: int32 [1024, 2], P('ex'), may hold values from 0 to 127, as said below
Outputs:
- gram: float32 [1024, 128, 128], P(('ex', 'lay'))
Inputs may be any that keep to these rules, and one draw needn't show every extreme that they name: Each device's listed first blocks are its own: pairs[p, 0] lies in 8 * (p // 64) to 8 * (p // 64 + 1) - 1. pairs[p, 1] is a device number of ex. The 64 pairs of one device are distinct and name every device number at least once. `prec_in`: each matrix has a diagonal between 1.5 and 6 and exceeds the sum of magnitudes of the rest of its row. `prec_out`: each matrix has a diagonal between 1.5 and 6 and exceeds the sum of magnitudes of the rest of its row.
All inputs are finite; a program needn't handle non-finite values.
Results may differ from a plain program's by a relative error of at most 0.0026.
Values may be sent and summed in bfloat16 or wider, within the bound.
No kernel may reach another device: no remote copies, remote signals or barrier semaphores. Data moves between devices by JAX's collectives and lax.ppermute only.
A program may use at most 128 MiB of HBM per device.

v0:
```python
import jax
import jax.numpy as jnp
from jax import lax
from jax.sharding import PartitionSpec as P

BLOCK = 128


def precondition(grads, prec_in, prec_out):
    layer_count, example_rows, width = grads.shape
    rank = prec_in.shape[-1]
    turned = jnp.swapaxes(grads, 1, 2).reshape(layer_count, rank, rank, example_rows)
    inner = jnp.einsum(
        "loie,lij->loje", turned, prec_in, preferred_element_type=jnp.float32
    ).astype(jnp.bfloat16)
    outer = jnp.einsum("lpo,loje->lpje", prec_out, inner, preferred_element_type=jnp.float32)
    return outer.astype(jnp.bfloat16).reshape(layer_count, width, example_rows)


def pick_tiles(products, first, source):
    return products[first, :, source, :]


def on_device(grads, prec_in, prec_out, requests, pairs):
    layer_count, example_rows, width = grads.shape
    blocks = grads.reshape(layer_count, example_rows // BLOCK, BLOCK, width)
    block_count = blocks.shape[1]
    member = lax.axis_index("ex")
    wanted = lax.dynamic_index_in_dim(requests, member, axis=1, keepdims=False)
    outgoing = jnp.take(blocks, wanted, axis=1)
    incoming = lax.all_to_all(outgoing, "ex", split_axis=1, concat_axis=1, tiled=True)
    holders = incoming.shape[1]
    left = precondition(grads, prec_in, prec_out)
    right = incoming.reshape(layer_count, holders * BLOCK, width)
    products = jnp.einsum("lqx,lmq->xm", left, right, preferred_element_type=jnp.float32)
    products = products.reshape(block_count, BLOCK, holders, BLOCK)
    first = pairs[:, 0] - member * block_count
    source = pairs[:, 1]
    pair_count = pairs.shape[0]
    share = pair_count // lax.axis_size("lay")
    terms = pick_tiles(products, first, source)
    total = lax.psum(terms, "lay")
    return lax.dynamic_slice_in_dim(total, lax.axis_index("lay") * share, share, 0)


def solution(mesh):
    placed = (P("lay", "ex", None), P("lay", None, None), P("lay", None, None), P(), P("ex", None))
    return jax.shard_map(
        on_device,
        mesh=mesh,
        in_specs=placed,
        out_specs=P(("ex", "lay"), None, None),
        check_vma=False,
    )
```

profile of v0, /device:TPU:0, one launch (start us, length us, event | category | flops | bytes accessed | tf_op | source)
XLA Modules:
  0.0 400.7 jit_solution(12002217262961592764)
XLA Ops:
  6.5 0.0 copy-start
  6.5 0.9 fusion.8
  7.4 0.9 and_reduce_fusion
  8.3 10.5 %gather_fusion = bf16[16,128,4096]{2,1,0:T(8,128)(2,1)} fusion(bf16[8,128,4096]{2,1,0:T(8,128)(2,1)} %bitcast.39, s32[1024]{0:T(1024)S(1)} %pad_clamp_fusion), kind=kCustom, calls=%fused_computation | custom fusion | bytes 33554496 | tf_op jit(solution)/shard_map/jit(_take)/gather | solution.py:30
  18.8 14.2 %bitcast_select_fusion = bf16[1,16,128,4096]{3,2,0,1:T(8,128)(2,1)} fusion(bf16[16,128,4096]{2,1,0:T(8,128)(2,1)} %gather_fusion, pred[16]{0:T(512)(128)(4,1)S(1)} %and_reduce_fusion), kind=kLoop, calls=%fused_computation.4 | loop fusion | flops 8388608 | bytes 33554448 | tf_op jit(solution)/shard_map/jit(_take)/select_n | solution.py:30
  33.0 7.2 %all-to-all-start = ((bf16[1,16,128,4096]{3,2,0,1:T(8,128)(2,1)}), bf16[1,16,128,4096]{3,2,0,1:T(8,128)(2,1)}, u32[]{:S(2)}, u32[]{:S(2)}) async-start(bf16[1,16,128,4096]{3,2,0,1:T(8,128)(2,1)} %bitcast_select_fusion), calls=%async_computation | async-start | bytes 33554432 | tf_op jit(solution)/shard_map/all_to_all | solution.py:31
  40.2 0.0 all-reduce.2.cloned.1.call-start
  40.3 12.0 %copy.14 = bf16[1,1024,4096]{1,2,0:T(8,128)(2,1)} copy(bf16[1,1024,4096]{2,1,0:T(8,128)(2,1)} %param.5) | data formatting | bytes 16777216 | tf_op args[0]
  52.2 0.0 copy-done
  52.2 0.0 copy-start.2
  52.2 5.8 %convert_bitcast_fusion.1 = bf16[64,64,1024]{2,1,0:T(8,128)(2,1)S(1)} fusion(bf16[64,64,1024]{2,1,0:T(8,128)(2,1)} %bitcast.40, bf16[1,64,64]{2,1,0:T(8,128)(2,1)S(1)} %copy-done), kind=kOutput, calls=%fused_computation.8 | convolution fusion | flops 541065216 | bytes 16785408 | tf_op jit(solution)/shard_map/loie,lij->loje/dot_general | solution.py:13
  58.0 0.0 copy-done.2
  58.0 12.9 %convert_bitcast_fusion = bf16[64,64,1024]{2,0,1:T(8,128)(2,1)} fusion(bf16[64,64,1024]{2,1,0:T(8,128)(2,1)S(1)} %convert_bitcast_fusion.1, bf16[1,64,64]{2,1,0:T(8,128)(2,1)S(1)} %copy-done.2), kind=kOutput, calls=%fused_computation.7 | convolution fusion | flops 541065216 | bytes 16785408 | tf_op jit(solution)/shard_map/lpo,loje->lpje/dot_general | solution.py:16
  70.9 11.3 %copy.17 = bf16[64,64,1024]{2,1,0:T(8,128)(2,1)} copy(bf16[64,64,1024]{2,0,1:T(8,128)(2,1)} %convert_bitcast_fusion) | data formatting | bytes 16777216 | tf_op jit(solution)/shard_map/convert_element_type | solution.py:17
  82.2 11.2 %copy.22 = bf16[1024,4096]{1,0:T(8,128)(2,1)} copy(bf16[1024,4096]{0,1:T(8,128)(2,1)} %bitcast.41) | data formatting | bytes 16777216 | tf_op jit(solution)/shard_map/lqx,lmq->xm/dot_general | solution.py:35
  93.4 0.0 copy-done.3
  93.4 196.5 %all-to-all-done = bf16[1,16,128,4096]{3,2,0,1:T(8,128)(2,1)} async-done(((bf16[1,16,128,4096]{3,2,0,1:T(8,128)(2,1)}), bf16[1,16,128,4096]{3,2,0,1:T(8,128)(2,1)}, u32[]{:S(2)}, u32[]{:S(2)}) %all-to-all-start) | async-done | bytes 16777248 | tf_op jit(solution)/shard_map/all_to_all | solution.py:31
  289.9 0.0 copy-start.1
  289.9 24.1 %fusion = f32[8,128,16,128]{3,1,2,0:T(8,128)} fusion(bf16[8,128,4096,1]{2,1,3,0:T(8,128)(2,1)} %bitcast.42, bf16[1,16,128,4096]{3,2,0,1:T(8,128)(2,1)} %all-to-all-done), kind=kOutput, calls=%fused_computation.2 | convolution fusion | flops 17179869184 | bytes 33554432 | tf_op jit(solution)/shard_map/lqx,lmq->xm/dot_general | solution.py:35
  314.0 6.1 %gather_fusion.1 = f32[64,128,128]{2,1,0:T(8,128)} fusion(f32[8,128,16,128]{3,1,2,0:T(8,128)} %fusion, s32[64]{0:T(128)S(1)} %fusion.14), kind=kCustom, calls=%fused_computation.1 | custom fusion | bytes 8389120 | tf_op jit(solution)/shard_map/gather | solution.py:21
  320.2 0.0 all-reduce.2.cloned.1.call-update
  320.2 71.8 %all-reduce.2.cloned.1.call-done = f32[64,128,128]{2,1,0:T(8,128)} async-done(((f32[64,128,128]{2,1,0:T(8,128)}), f32[64,128,128]{2,1,0:T(8,128)}) %all-reduce.2.cloned.1.call-update) | async-done | bytes 4194320 | tf_op jit(solution)/shard_map/psum | solution.py:42
  392.0 1.9 constant_dynamic-slice_fusion
  393.9 0.0 copy-done.1
  (3 shorter events, 0.0 us)
Async XLA Ops:
  6.5 45.7 %copy-start = (bf16[1,64,64]{2,1,0:T(8,128)(2,1)S(1)}, bf16[1,64,64]{2,1,0:T(8,128)(2,1)}, u32[]{:S(2)}) copy-start(bf16[1,64,64]{2,1,0:T(8,128)(2,1)} %param.6) | copy-start | bytes 24580
  33.0 257.0 %all-to-all-start = ((bf16[1,16,128,4096]{3,2,0,1:T(8,128)(2,1)}), bf16[1,16,128,4096]{3,2,0,1:T(8,128)(2,1)}, u32[]{:S(2)}, u32[]{:S(2)}) async-start(bf16[1,16,128,4096]{3,2,0,1:T(8,128)(2,1)} %bitcast_select_fusion), calls=%async_computation | async-start | bytes 33554432 | tf_op jit(solution)/shard_map/all_to_all | solution.py:31
  40.2 351.8 %all-reduce.2.cloned.1.call-start = ((), (), s32[]{:S(2)}) async-start(), calls=%async_computation.1 | async-start | bytes 8388608 | tf_op jit(solution)/shard_map/psum | solution.py:42
  52.2 5.8 %copy-start.2 = (bf16[1,64,64]{2,1,0:T(8,128)(2,1)S(1)}, bf16[1,64,64]{2,1,0:T(8,128)(2,1)}, u32[]{:S(2)}) copy-start(bf16[1,64,64]{2,1,0:T(8,128)(2,1)} %param.7) | copy-start | bytes 24580
  82.2 11.2 %copy-start.3 = (s32[64,2]{0,1:T(2,128)S(1)}, s32[64,2]{0,1:T(2,128)}, u32[]{:S(2)}) copy-start(s32[64,2]{0,1:T(2,128)} %param.9) | copy-start | bytes 1540
  289.9 103.9 %copy-start.1 = (bf16[1,64,64]{2,1,0:T(8,128)(2,1)S(1)}, bf16[1,64,64]{2,1,0:T(8,128)(2,1)}, u32[]{:S(2)}) copy-start(bf16[1,64,64]{2,1,0:T(8,128)(2,1)} %param.6) | copy-start | bytes 24580
Sparse Core Ops, SparseCore 0:
  320.3 71.6 all-reduce.1
where the time goes:
time: 402 us; the launch traced here: 401 us
  waiting for transfers between devices  268 us (67%)
  local copies, waits for them, and re-layouts  53 us (13%)
  matrix products  42.8 us (11%)
  other arithmetic  15.9 us (4%)
  between operations  13.4 us (3%)
  starting transfers between devices  7.28 us (2%)
    all_to_all x1, waiting for transfers between devices, on_device(): lax.all_to_all(outgoing, 'ex', split_axis=1, concat_axis=1, tiled=True)  197 us
    psum x1, waiting for transfers between devices, on_device(): total = lax.psum(terms, 'lay')  71.8 us
    dot_general x1, matrix products, on_device(): jnp.einsum('lqx,lmq->xm', left, right, preferred_element_type=jnp.float32)  24.1 us
    select_n x2, other arithmetic, on_device(): outgoing = jnp.take(blocks, wanted, axis=1)  15 us
    dot_general x1, matrix products, precondition(): jnp.einsum('lpo,loje->lpje', prec_out, inner, preferred_element_type=jnp....  12.9 us
    unnamed x9, local copies, waits for them, and re-layouts  12 us
    convert_element_type x1, local copies, waits for them, and re-layouts, precondition(): return outer.astype(jnp.bfloat16).reshape(layer_count, width, example_rows)  11.3 us
    dot_general x1, local copies, waits for them, and re-layouts, on_device(): jnp.einsum('lqx,lmq->xm', left, right, preferred_element_type=jnp.float32)  11.2 us
  transfers between devices with their start and end apart: 2, of which 2 were waited for; matrix products, arithmetic and copies ran while one was open for 13% of the time, Pallas kernels for 0%

commit v1 on v0

--- a/solution.py
+++ b/solution.py
@@ -4,6 +4,18 @@
 from jax.sharding import PartitionSpec as P
 
 BLOCK = 128
+
+
+def rotated_exchange(array, axis, split, join):
+    ways, here = (lax.axis_size(axis), lax.axis_index(axis))
+    width = array.shape[split] // ways
+    turned = jnp.roll(array, -here * width, axis=split)
+    got = [lax.slice_in_dim(turned, 0, width, axis=split)]
+    for far in range(1, ways):
+        sent = lax.slice_in_dim(turned, far * width, (far + 1) * width, axis=split)
+        got.append(lax.ppermute(sent, axis, [(d, (d + far) % ways) for d in range(ways)]))
+    line = jnp.concatenate(got[::-1], axis=join)
+    return jnp.roll(line, (here + 1) * got[0].shape[join], axis=join)
 
 
 def precondition(grads, prec_in, prec_out):
@@ -28,7 +40,7 @@
     member = lax.axis_index("ex")
     wanted = lax.dynamic_index_in_dim(requests, member, axis=1, keepdims=False)
     outgoing = jnp.take(blocks, wanted, axis=1)
-    incoming = lax.all_to_all(outgoing, "ex", split_axis=1, concat_axis=1, tiled=True)
+    incoming = rotated_exchange(outgoing, "ex", 1, 1)
     holders = incoming.shape[1]
     left = precondition(grads, prec_in, prec_out)
     right = incoming.reshape(layer_count, holders * BLOCK, width)

time: 402 us -> 506 us (1.26)
  starting transfers between devices: 7.28 us -> 178 us
  waiting for transfers between devices: 268 us -> 147 us
  local copies, waits for them, and re-layouts: 53 us -> 87.9 us
  other arithmetic: 15.9 us -> 26.6 us
  matrix products: 42.8 us -> 51.1 us
    all_to_all x1 -> x0, waiting for transfers between devices: 197 us -> none  [on_device(): lax.all_to_all(outgoing, 'ex', split_axis=1, concat_axis=1, tiled=True)]
    ppermute x0 -> x15, starting transfers between devices: none -> 178 us  [rotated_exchange(): lax.ppermute(sent, axis, [(d, (d + far) % ways) for d in range(ways)])]
    ppermute x0 -> x15, waiting for transfers between devices: none -> 74.8 us  [rotated_exchange(): lax.ppermute(sent, axis, [(d, (d + far) % ways) for d in range(ways)])]
    unnamed x9 -> x30, local copies, waits for them, and re-layouts: 12 us -> 40 us
    concatenate x0 -> x1, other arithmetic: none -> 10.6 us  [rotated_exchange(): turned = jnp.roll(array, -here * width, axis=split)]
    all_to_all x1 -> x0, starting transfers between devices: 7.24 us -> none  [on_device(): lax.all_to_all(outgoing, 'ex', split_axis=1, concat_axis=1, tiled=True)]
  transfers between devices with their start and end apart: 2 -> 16, of which waited for: 2 -> 3; matrix products, arithmetic and copies ran while one was open for 13% -> 16% of each run, Pallas kernels for 0% -> 0%
where the time goes in v1:
time: 506 us; the launch traced here: 504 us
  starting transfers between devices  178 us (35%)
  waiting for transfers between devices  147 us (29%)
  local copies, waits for them, and re-layouts  87.9 us (17%)
  matrix products  51.1 us (10%)
  other arithmetic  26.6 us (5%)
  between operations  13.5 us (3%)
    ppermute x15, starting transfers between devices, rotated_exchange(): lax.ppermute(sent, axis, [(d, (d + far) % ways) for d in range(ways)])  178 us
    ppermute x15, waiting for transfers between devices, rotated_exchange(): lax.ppermute(sent, axis, [(d, (d + far) % ways) for d in range(ways)])  74.8 us
    psum x1, waiting for transfers between devices, on_device(): total = lax.psum(terms, 'lay')  72.2 us
    unnamed x30, local copies, waits for them, and re-layouts  40 us
    dot_general x1, matrix products, on_device(): jnp.einsum('lqx,lmq->xm', left, right, preferred_element_type=jnp.float32)  24.2 us
    dot_general x1, matrix products, precondition(): jnp.einsum('lpo,loje->lpje', prec_out, inner, preferred_element_type=jnp....  17.8 us
    select_n x2, other arithmetic, on_device(): outgoing = jnp.take(blocks, wanted, axis=1)  15 us
    convert_element_type x1, local copies, waits for them, and re-layouts, precondition(): return outer.astype(jnp.bfloat16).reshape(layer_count, width, example_rows)  11.3 us
  transfers between devices with their start and end apart: 16, of which 3 were waited for; matrix products, arithmetic and copies ran while one was open for 16% of the time, Pallas kernels for 0%

profile of v1, /device:TPU:0, one launch (start us, length us, event | category | flops | bytes accessed | tf_op | source)
XLA Modules:
  0.0 504.3 jit_solution(9517750045782320763)
XLA Ops:
  8.3 10.5 %gather_fusion = bf16[16,128,4096]{2,1,0:T(8,128)(2,1)} fusion(bf16[8,128,4096]{2,1,0:T(8,128)(2,1)} %bitcast.39, s32[1024]{0:T(1024)S(1)} %pad_clamp_fusion), kind=kCustom, calls=%fused_computation | custom fusion | bytes 33554496 | tf_op jit(solution)/shard_map/jit(_take)/gather | solution.py:42
  18.9 14.1 %bitcast_select_fusion = bf16[1,16,128,4096]{3,2,1,0:T(8,128)(2,1)} fusion(bf16[16,128,4096]{2,1,0:T(8,128)(2,1)} %gather_fusion, pred[16]{0:T(512)(128)(4,1)S(1)} %and_reduce_fusion), kind=kLoop, calls=%fused_computation.10 | loop fusion | flops 8388608 | bytes 33554448 | tf_op jit(solution)/shard_map/jit(_take)/select_n | solution.py:42
  33.0 10.6 %fusion.4 = bf16[1,16,128,4096]{3,2,1,0:T(8,128)(2,1)S(1)} fusion(s32[]{:T(128)S(6)} %select_n.53, bf16[1,16,128,4096]{3,2,1,0:T(8,128)(2,1)} %bitcast_select_fusion), kind=kLoop, calls=%fused_computation.9 | loop fusion | flops 8388608 | bytes 33554436 | tf_op jit(solution)/shard_map/jit(_roll_dynamic)/concatenate | solution.py:12
  43.7 5.7 %copy-done.2 = bf16[1,16,128,4096]{3,2,1,0:T(8,128)(2,1)} copy-done((bf16[1,16,128,4096]{3,2,1,0:T(8,128)(2,1)}, bf16[1,16,128,4096]{3,2,1,0:T(8,128)(2,1)S(1)}, u32[]{:S(2)}) %copy-start.2) | copy-done | bytes 16777240
  49.4 4.5 fusion.20
  53.9 5.4 %collective-permute-start = (bf16[1,1,128,4096]{3,2,1,0:T(8,128)(2,1)}, bf16[1,1,128,4096]{3,2,1,0:T(8,128)(2,1)}, u32[]{:S(2)}, u32[]{:S(2)}) collective-permute-start(bf16[1,1,128,4096]{3,2,1,0:T(8,128)(2,1)} %get-tuple-element.20), channel_id=1, source_target_pairs={{0,120},{8,0},{16,8},{24,16},{32,24},{40,32},{48,40},{56,48},{64,5... | collective-permute-start | bytes 3145736 | tf_op jit(solution)/shard_map/ppermute | solution.py:16
  63.7 11.9 %copy.9 = bf16[1,1024,4096]{1,2,0:T(8,128)(2,1)} copy(bf16[1,1024,4096]{2,1,0:T(8,128)(2,1)} %param.7) | data formatting | bytes 16777216 | tf_op args[0]
  75.6 9.0 %convert_bitcast_fusion.1 = bf16[64,64,1024]{2,1,0:T(8,128)(2,1)} fusion(bf16[64,64,1024]{2,1,0:T(8,128)(2,1)} %bitcast.40, bf16[1,64,64]{2,1,0:T(8,128)(2,1)S(1)} %copy-done), kind=kOutput, calls=%fused_computation.14 | convolution fusion | flops 541065216 | bytes 16785408 | tf_op jit(solution)/shard_map/loie,lij->loje/dot_general | solution.py:25
  84.6 17.8 %convert_bitcast_fusion = bf16[64,64,1024]{2,0,1:T(8,128)(2,1)} fusion(bf16[64,64,1024]{2,1,0:T(8,128)(2,1)} %convert_bitcast_fusion.1, bf16[1,64,64]{2,1,0:T(8,128)(2,1)S(1)} %copy-done.3), kind=kOutput, calls=%fused_computation.13 | convolution fusion | flops 541065216 | bytes 16785408 | tf_op jit(solution)/shard_map/lpo,loje->lpje/dot_general | solution.py:28
  102.5 11.3 %copy.12 = bf16[64,64,1024]{2,1,0:T(8,128)(2,1)} copy(bf16[64,64,1024]{2,0,1:T(8,128)(2,1)} %convert_bitcast_fusion) | data formatting | bytes 16777216 | tf_op jit(solution)/shard_map/convert_element_type | solution.py:29
  113.8 11.3 %copy.17 = bf16[1024,4096]{1,0:T(8,128)(2,1)} copy(bf16[1024,4096]{0,1:T(8,128)(2,1)} %bitcast.41) | data formatting | bytes 16777216 | tf_op jit(solution)/shard_map/lqx,lmq->xm/dot_general | solution.py:47
  125.1 4.2 collective-permute-start.5
  138.4 81.4 %collective-permute-start.8 = (bf16[1,1,128,4096]{3,2,1,0:T(8,128)(2,1)}, bf16[1,1,128,4096]{3,2,1,0:T(8,128)(2,1)S(1)}, u32[]{:S(2)}, u32[]{:S(2)}) collective-permute-start(bf16[1,1,128,4096]{3,2,1,0:T(8,128)(2,1)} %get-tuple-element.12), channel_id=1, source_target_pairs={{0,56},{8,64},{16,72},{24,80},{32,88},{40,96},{48,104},{56,112},{6... | collective-permute-start | bytes 3145736 | tf_op jit(solution)/shard_map/ppermute | solution.py:16
  219.9 2.3 constant_dynamic-update-slice_fusion.11
  224.5 3.6 collective-permute-start.10
  229.2 23.3 %collective-permute-start.11 = (bf16[1,1,128,4096]{3,2,1,0:T(8,128)(2,1)}, bf16[1,1,128,4096]{3,2,1,0:T(8,128)(2,1)S(1)}, u32[]{:S(2)}, u32[]{:S(2)}) collective-permute-start(bf16[1,1,128,4096]{3,2,1,0:T(8,128)(2,1)} %get-tuple-element.9), channel_id=1, source_target_pairs={{0,32},{8,40},{16,48},{24,56},{32,64},{40,72},{48,80},{56,88},{64,... | collective-permute-start | bytes 3145736 | tf_op jit(solution)/shard_map/ppermute | solution.py:16
  253.6 2.4 collective-permute-start.12
  257.1 9.1 %collective-permute-done.8 = bf16[1,1,128,4096]{3,2,1,0:T(8,128)(2,1)S(1)} collective-permute-done((bf16[1,1,128,4096]{3,2,1,0:T(8,128)(2,1)}, bf16[1,1,128,4096]{3,2,1,0:T(8,128)(2,1)S(1)}, u32[]{:S(2)}, u32[]{:S(2)}) %collective-permute-start.8) | collective-permute-done | bytes 1048608 | tf_op jit(solution)/shard_map/ppermute | solution.py:16
  267.4 51.1 %collective-permute-start.14 = (bf16[1,1,128,4096]{3,2,1,0:T(8,128)(2,1)S(1)}, bf16[1,1,128,4096]{3,2,1,0:T(8,128)(2,1)S(1)}, u32[]{:S(2)}, u32[]{:S(2)}) collective-permute-start(bf16[1,1,128,4096]{3,2,1,0:T(8,128)(2,1)S(1)} %get-tuple-element.6), channel_id=1, source_target_pairs={{0,8},{8,16},{16,24},{24,32},{32,40},{40,48},{48,56},{56,64},{64,7... | collective-permute-start | bytes 3145736 | tf_op jit(solution)/shard_map/ppermute | solution.py:16
  320.6 65.6 %collective-permute-done.11 = bf16[1,1,128,4096]{3,2,1,0:T(8,128)(2,1)S(1)} collective-permute-done((bf16[1,1,128,4096]{3,2,1,0:T(8,128)(2,1)}, bf16[1,1,128,4096]{3,2,1,0:T(8,128)(2,1)S(1)}, u32[]{:S(2)}, u32[]{:S(2)}) %collective-permute-start.11) | collective-permute-done | bytes 1048608 | tf_op jit(solution)/shard_map/ppermute | solution.py:16
  390.6 2.3 slice_dynamic-update-slice_fusion
  392.9 24.2 %fusion.2 = f32[8,128,16,128]{3,1,2,0:T(8,128)} fusion(bf16[8,128,4096,1]{2,1,3,0:T(8,128)(2,1)S(1)} %bitcast.44, s32[]{:T(128)S(6)} %select_n.55, bf16[1,16,128,4096]{3,2,1,0:T(8,128)(2,1)} %slice_dynamic-update-slice_fusion), kind=kOutput, calls=%fused_computation.8 | convolution fusion | flops 17213423616 | bytes 33554436 | tf_op jit(solution)/shard_map/lqx,lmq->xm/dot_general | solution.py:47
  417.2 6.2 %gather_fusion.1 = f32[64,128,128]{2,1,0:T(8,128)} fusion(f32[8,128,16,128]{3,1,2,0:T(8,128)} %fusion.2, s32[64]{0:T(128)S(1)} %fusion.18), kind=kCustom, calls=%fused_computation.1 | custom fusion | bytes 8389120 | tf_op jit(solution)/shard_map/gather | solution.py:33
  423.4 72.2 %all-reduce.2.cloned.1.call-done = f32[64,128,128]{2,1,0:T(8,128)} async-done(((f32[64,128,128]{2,1,0:T(8,128)}), f32[64,128,128]{2,1,0:T(8,128)}) %all-reduce.2.cloned.1.call-update) | async-done | bytes 4194320 | tf_op jit(solution)/shard_map/psum | solution.py:54
  (56 shorter events, 30.4 us)
Async XLA Ops:
  6.5 69.1 %copy-start = (bf16[1,64,64]{2,1,0:T(8,128)(2,1)S(1)}, bf16[1,64,64]{2,1,0:T(8,128)(2,1)}, u32[]{:S(2)}) copy-start(bf16[1,64,64]{2,1,0:T(8,128)(2,1)} %param.8) | copy-start | bytes 24580
  6.5 489.0 %all-reduce.2.cloned.1.call-start = ((), (), s32[]{:S(2)}) async-start(), calls=%async_computation | async-start | bytes 8388608 | tf_op jit(solution)/shard_map/psum | solution.py:54
  43.6 5.7 %copy-start.2 = (bf16[1,16,128,4096]{3,2,1,0:T(8,128)(2,1)}, bf16[1,16,128,4096]{3,2,1,0:T(8,128)(2,1)S(1)}, u32[]{:S(2)}) copy-start(bf16[1,16,128,4096]{3,2,1,0:T(8,128)(2,1)S(1)} %fusion.4) | copy-start | bytes 50331652
  53.9 71.2 %collective-permute-start = (bf16[1,1,128,4096]{3,2,1,0:T(8,128)(2,1)}, bf16[1,1,128,4096]{3,2,1,0:T(8,128)(2,1)}, u32[]{:S(2)}, u32[]{:S(2)}) collective-permute-start(bf16[1,1,128,4096]{3,2,1,0:T(8,128)(2,1)} %get-tuple-element.20), channel_id=1, source_target_pairs={{0,120},{8,0},{16,8},{24,16},{32,24},{40,32},{48,40},{56,48},{64,5... | collective-permute-start | bytes 3145736 | tf_op jit(solution)/shard_map/ppermute | solution.py:16
  59.3 72.3 %collective-permute-start.1 = (bf16[1,1,128,4096]{3,2,1,0:T(8,128)(2,1)}, bf16[1,1,128,4096]{3,2,1,0:T(8,128)(2,1)}, u32[]{:S(2)}, u32[]{:S(2)}) collective-permute-start(bf16[1,1,128,4096]{3,2,1,0:T(8,128)(2,1)} %get-tuple-element.19), channel_id=1, source_target_pairs={{0,112},{8,120},{16,0},{24,8},{32,16},{40,24},{48,32},{56,40},{64,... | collective-permute-start | bytes 3145736 | tf_op jit(solution)/shard_map/ppermute | solution.py:16
  60.1 73.9 %collective-permute-start.2 = (bf16[1,1,128,4096]{3,2,1,0:T(8,128)(2,1)}, bf16[1,1,128,4096]{3,2,1,0:T(8,128)(2,1)}, u32[]{:S(2)}, u32[]{:S(2)}) collective-permute-start(bf16[1,1,128,4096]{3,2,1,0:T(8,128)(2,1)} %get-tuple-element.18), channel_id=1, source_target_pairs={{0,104},{8,112},{16,120},{24,0},{32,8},{40,16},{48,24},{56,32},{64... | collective-permute-start | bytes 3145736 | tf_op jit(solution)/shard_map/ppermute | solution.py:16
  61.1 77.3 %collective-permute-start.3 = (bf16[1,1,128,4096]{3,2,1,0:T(8,128)(2,1)}, bf16[1,1,128,4096]{3,2,1,0:T(8,128)(2,1)}, u32[]{:S(2)}, u32[]{:S(2)}) collective-permute-start(bf16[1,1,128,4096]{3,2,1,0:T(8,128)(2,1)} %get-tuple-element.17), channel_id=1, source_target_pairs={{0,96},{8,104},{16,112},{24,120},{32,0},{40,8},{48,16},{56,24},{64... | collective-permute-start | bytes 3145736 | tf_op jit(solution)/shard_map/ppermute | solution.py:16
  61.5 23.1 %copy-start.3 = (bf16[1,64,64]{2,1,0:T(8,128)(2,1)S(1)}, bf16[1,64,64]{2,1,0:T(8,128)(2,1)}, u32[]{:S(2)}) copy-start(bf16[1,64,64]{2,1,0:T(8,128)(2,1)} %param.9) | copy-start | bytes 24580
  61.5 160.6 %collective-permute-start.4 = (bf16[1,1,128,4096]{3,2,1,0:T(8,128)(2,1)}, bf16[1,1,128,4096]{3,2,1,0:T(8,128)(2,1)}, u32[]{:S(2)}, u32[]{:S(2)}) collective-permute-start(bf16[1,1,128,4096]{3,2,1,0:T(8,128)(2,1)} %get-tuple-element.16), channel_id=1, source_target_pairs={{0,88},{8,96},{16,104},{24,112},{32,120},{40,0},{48,8},{56,16},{64... | collective-permute-start | bytes 3145736 | tf_op jit(solution)/shard_map/ppermute | solution.py:16
  75.6 26.9 %copy-start.4 = (s32[64,2]{0,1:T(2,128)S(1)}, s32[64,2]{0,1:T(2,128)}, u32[]{:S(2)}) copy-start(s32[64,2]{0,1:T(2,128)} %param.11) | copy-start | bytes 1540
  125.1 267.8 %slice-start = ((s8[8388608]{0:T(1024)(128)(4,1)}), s8[4194304]{0:T(1024)(128)(4,1)S(1)}, s32[]{:S(2)}) async-start(s8[8388608]{0:T(1024)(128)(4,1)} %bitcast.42), calls=%async_computation.1 | async-start | bytes 8388608
  125.1 99.4 %collective-permute-start.5 = (bf16[1,1,128,4096]{3,2,1,0:T(8,128)(2,1)}, bf16[1,1,128,4096]{3,2,1,0:T(8,128)(2,1)S(1)}, u32[]{:S(2)}, u32[]{:S(2)}) collective-permute-start(bf16[1,1,128,4096]{3,2,1,0:T(8,128)(2,1)} %get-tuple-element.15), channel_id=1, source_target_pairs={{0,80},{8,88},{16,96},{24,104},{32,112},{40,120},{48,0},{56,8},{64... | collective-permute-start | bytes 3145736 | tf_op jit(solution)/shard_map/ppermute | solution.py:16
  131.6 97.6 %collective-permute-start.6 = (bf16[1,1,128,4096]{3,2,1,0:T(8,128)(2,1)}, bf16[1,1,128,4096]{3,2,1,0:T(8,128)(2,1)S(1)}, u32[]{:S(2)}, u32[]{:S(2)}) collective-permute-start(bf16[1,1,128,4096]{3,2,1,0:T(8,128)(2,1)} %get-tuple-element.14), channel_id=1, source_target_pairs={{0,72},{8,80},{16,88},{24,96},{32,104},{40,112},{48,120},{56,0},{6... | collective-permute-start | bytes 3145736 | tf_op jit(solution)/shard_map/ppermute | solution.py:16
  133.9 119.7 %collective-permute-start.7 = (bf16[1,1,128,4096]{3,2,1,0:T(8,128)(2,1)}, bf16[1,1,128,4096]{3,2,1,0:T(8,128)(2,1)S(1)}, u32[]{:S(2)}, u32[]{:S(2)}) collective-permute-start(bf16[1,1,128,4096]{3,2,1,0:T(8,128)(2,1)} %get-tuple-element.13), channel_id=1, source_target_pairs={{0,64},{8,72},{16,80},{24,88},{32,96},{40,104},{48,112},{56,120},{... | collective-permute-start | bytes 3145736 | tf_op jit(solution)/shard_map/ppermute | solution.py:16
  138.4 127.8 %collective-permute-start.8 = (bf16[1,1,128,4096]{3,2,1,0:T(8,128)(2,1)}, bf16[1,1,128,4096]{3,2,1,0:T(8,128)(2,1)S(1)}, u32[]{:S(2)}, u32[]{:S(2)}) collective-permute-start(bf16[1,1,128,4096]{3,2,1,0:T(8,128)(2,1)} %get-tuple-element.12), channel_id=1, source_target_pairs={{0,56},{8,64},{16,72},{24,80},{32,88},{40,96},{48,104},{56,112},{6... | collective-permute-start | bytes 3145736 | tf_op jit(solution)/shard_map/ppermute | solution.py:16
  222.2 45.2 %collective-permute-start.9 = (bf16[1,1,128,4096]{3,2,1,0:T(8,128)(2,1)}, bf16[1,1,128,4096]{3,2,1,0:T(8,128)(2,1)S(1)}, u32[]{:S(2)}, u32[]{:S(2)}) collective-permute-start(bf16[1,1,128,4096]{3,2,1,0:T(8,128)(2,1)} %get-tuple-element.11), channel_id=1, source_target_pairs={{0,48},{8,56},{16,64},{24,72},{32,80},{40,88},{48,96},{56,104},{64... | collective-permute-start | bytes 3145736 | tf_op jit(solution)/shard_map/ppermute | solution.py:16
  224.5 95.1 %collective-permute-start.10 = (bf16[1,1,128,4096]{3,2,1,0:T(8,128)(2,1)}, bf16[1,1,128,4096]{3,2,1,0:T(8,128)(2,1)S(1)}, u32[]{:S(2)}, u32[]{:S(2)}) collective-permute-start(bf16[1,1,128,4096]{3,2,1,0:T(8,128)(2,1)} %get-tuple-element.10), channel_id=1, source_target_pairs={{0,40},{8,48},{16,56},{24,64},{32,72},{40,80},{48,88},{56,96},{64,... | collective-permute-start | bytes 3145736 | tf_op jit(solution)/shard_map/ppermute | solution.py:16
  229.2 157.1 %collective-permute-start.11 = (bf16[1,1,128,4096]{3,2,1,0:T(8,128)(2,1)}, bf16[1,1,128,4096]{3,2,1,0:T(8,128)(2,1)S(1)}, u32[]{:S(2)}, u32[]{:S(2)}) collective-permute-start(bf16[1,1,128,4096]{3,2,1,0:T(8,128)(2,1)} %get-tuple-element.9), channel_id=1, source_target_pairs={{0,32},{8,40},{16,48},{24,56},{32,64},{40,72},{48,80},{56,88},{64,... | collective-permute-start | bytes 3145736 | tf_op jit(solution)/shard_map/ppermute | solution.py:16
  253.6 139.3 %slice-start.1 = ((s8[8388608]{0:T(1024)(128)(4,1)}), s8[4194304]{0:T(1024)(128)(4,1)S(1)}, s32[]{:S(2)}) async-start(s8[8388608]{0:T(1024)(128)(4,1)} %bitcast.42), calls=%async_computation.2 | async-start | bytes 8388608
  253.6 133.8 %collective-permute-start.12 = (bf16[1,1,128,4096]{3,2,1,0:T(8,128)(2,1)S(1)}, bf16[1,1,128,4096]{3,2,1,0:T(8,128)(2,1)S(1)}, u32[]{:S(2)}, u32[]{:S(2)}) collective-permute-start(bf16[1,1,128,4096]{3,2,1,0:T(8,128)(2,1)S(1)} %get-tuple-element.8), channel_id=1, source_target_pairs={{0,24},{8,32},{16,40},{24,48},{32,56},{40,64},{48,72},{56,80},{64,... | collective-permute-start | bytes 3145736 | tf_op jit(solution)/shard_map/ppermute | solution.py:16
  266.2 122.2 %collective-permute-start.13 = (bf16[1,1,128,4096]{3,2,1,0:T(8,128)(2,1)S(1)}, bf16[1,1,128,4096]{3,2,1,0:T(8,128)(2,1)S(1)}, u32[]{:S(2)}, u32[]{:S(2)}) collective-permute-start(bf16[1,1,128,4096]{3,2,1,0:T(8,128)(2,1)S(1)} %get-tuple-element.7), channel_id=1, source_target_pairs={{0,16},{8,24},{16,32},{24,40},{32,48},{40,56},{48,64},{56,72},{64,... | collective-permute-start | bytes 3145736 | tf_op jit(solution)/shard_map/ppermute | solution.py:16
  267.4 122.1 %collective-permute-start.14 = (bf16[1,1,128,4096]{3,2,1,0:T(8,128)(2,1)S(1)}, bf16[1,1,128,4096]{3,2,1,0:T(8,128)(2,1)S(1)}, u32[]{:S(2)}, u32[]{:S(2)}) collective-permute-start(bf16[1,1,128,4096]{3,2,1,0:T(8,128)(2,1)S(1)} %get-tuple-element.6), channel_id=1, source_target_pairs={{0,8},{8,16},{16,24},{24,32},{32,40},{40,48},{48,56},{56,64},{64,7... | collective-permute-start | bytes 3145736 | tf_op jit(solution)/shard_map/ppermute | solution.py:16
  392.9 104.5 %copy-start.1 = (bf16[1,64,64]{2,1,0:T(8,128)(2,1)S(1)}, bf16[1,64,64]{2,1,0:T(8,128)(2,1)}, u32[]{:S(2)}) copy-start(bf16[1,64,64]{2,1,0:T(8,128)(2,1)} %param.8) | copy-start | bytes 24580
Sparse Core Ops, SparseCore 0:
  423.5 72.0 all-reduce.1
